TPU v7x, 32 devices: a whole 2x2x4 slice. The times are simulated.
32 devices in a mesh: blk: 8 (over z, y), rep: 4 (over x, core).
Axes of the slice: x: 2, y: 2, z: 4, core: 2. Of those that a mesh axis runs over, the one named last changes fastest.
Arguments:
- feats: bfloat16 [8192, 256], P(('blk', 'rep')), may hold values from -6 to 6
- weight: bfloat16 [256, 256], replicated, may hold values from -0.375 to 0.375
- bias: float32 [256], replicated, may hold values from -4 to 4
- grad_out: bfloat16 [8192, 256], P(('blk', 'rep')), may hold values from -6 to 6
- tile_values: bfloat16 [8, 4, 2, 64, 128, 128], P('blk', 'rep'), may hold values from -0.0625 to 0.0625
- tile_rows: int32 [8, 4, 2, 64], P('blk', 'rep'), may hold values from 0 to 7, as said below
- tile_cols: int32 [8, 4, 2, 64], P('blk', 'rep'), may hold values from 0 to 7, as said below
- tile_count: int32 [8, 4, 2], P('blk', 'rep'), may hold values from 32 to 64, as said below
Outputs:
- out: bfloat16 [8192, 256], P(('blk', 'rep'))
- grad_feats: bfloat16 [8192, 256], P(('blk', 'rep'))
- grad_weight: float32 [256, 256], P('rep')
- grad_bias: float32 [256], replicated
Inputs may be any that keep to these rules, and one draw needn't show every extreme that they name: `tile_count`: some pair slot of some device holds exactly 64 live entries; slots past the count hold values that must be ignored. Within one pair slot the 64 entries name distinct (tile_rows, tile_cols) cells. `tile_cols`: see tile_rows: cells of one slot are distinct.
All inputs are finite; a program needn't handle non-finite values.
Results may differ from a plain program's by a relative error of at most 0.018.
Values may be sent and summed in bfloat16 or wider, within the bound.
A program may use at most 64 MiB of HBM per device.

v0:
```python
import jax
import jax.numpy as jnp
from jax import lax
from jax.sharding import PartitionSpec as P


def passed_along(x, axis, by):
    devices = lax.axis_size(axis)
    return lax.ppermute(x, axis, [(i, (i + by) % devices) for i in range(devices)])


def forward_tiles(total, source, tile_vals, tile_row, tile_col, live, tile_size):

    def forward_one_tile(position, total):
        row_start = tile_row[position] * tile_size
        col_start = tile_col[position] * tile_size
        source_rows = lax.dynamic_slice_in_dim(source, col_start, tile_size, 0)
        current = lax.dynamic_slice_in_dim(total, row_start, tile_size, 0)
        current = current + jnp.dot(
            tile_vals[position], source_rows, preferred_element_type=jnp.float32
        )
        return lax.dynamic_update_slice_in_dim(total, current, row_start, 0)

    return lax.fori_loop(0, live, forward_one_tile, total)


def backward_tiles(total, grad_block, tile_vals, tile_row, tile_col, live, tile_size):

    def backward_one_tile(position, total):
        row_start = tile_row[position] * tile_size
        col_start = tile_col[position] * tile_size
        grad_rows = lax.dynamic_slice_in_dim(grad_block, row_start, tile_size, 0)
        term = lax.dot_general(
            tile_vals[position],
            grad_rows,
            (((0,), (0,)), ((), ())),
            preferred_element_type=jnp.float32,
        )
        current = lax.dynamic_slice_in_dim(total, col_start, tile_size, 0)
        return lax.dynamic_update_slice_in_dim(total, current + term, col_start, 0)

    return lax.fori_loop(0, live, backward_one_tile, total)


def activation(pre_act, cotangent):
    logistic = jax.nn.sigmoid(pre_act)
    result = (pre_act * logistic).astype(jnp.bfloat16)
    grad_pre = (
        cotangent.astype(jnp.float32) * logistic * (1.0 + pre_act * (1.0 - logistic))
    ).astype(jnp.bfloat16)
    return (result, grad_pre)


def body(feats, weight, bias, grad_out, tile_values, tile_rows, tile_cols, tile_count):
    replicas = lax.axis_size("rep")
    rep_index = lax.axis_index("rep")
    tile_size = tile_values.shape[-1]
    pair_slots = tile_values.shape[2]
    digit_count = (replicas - 1).bit_length()
    values_here = tile_values[0, 0]
    rows_here = tile_rows[0, 0]
    cols_here = tile_cols[0, 0]
    counts_here = tile_count[0, 0]
    hw_slice = jnp.dot(feats, weight, preferred_element_type=jnp.float32).astype(jnp.bfloat16)
    feature_block = lax.all_gather(hw_slice, "rep", axis=0, tiled=True)
    for level in range(digit_count):
        shifted = passed_along(feature_block, "blk", 1 << level)
        feature_block = jnp.where(rep_index // (1 << level) % 2 == 1, shifted, feature_block)
    aggregate = jnp.zeros(feature_block.shape, jnp.float32)
    for slot in range(pair_slots):
        aggregate = forward_tiles(
            aggregate,
            feature_block,
            values_here[slot],
            rows_here[slot],
            cols_here[slot],
            counts_here[slot],
            tile_size,
        )
        if slot + 1 < pair_slots:
            feature_block = passed_along(feature_block, "blk", replicas)
    aggregate_rows = lax.psum_scatter(
        aggregate.astype(jnp.bfloat16), "rep", scatter_dimension=0, tiled=True
    ).astype(jnp.float32)
    out, grad_rows = activation(aggregate_rows + bias, grad_out)
    grad_block = lax.all_gather(grad_rows, "rep", axis=0, tiled=True)
    partial_grad = jnp.zeros(grad_block.shape, jnp.float32)
    for slot in reversed(range(pair_slots)):
        partial_grad = backward_tiles(
            partial_grad,
            grad_block,
            values_here[slot],
            rows_here[slot],
            cols_here[slot],
            counts_here[slot],
            tile_size,
        )
        if slot > 0:
            partial_grad = passed_along(partial_grad.astype(jnp.bfloat16), "blk", -replicas).astype(
                partial_grad.dtype
            )
    for level in reversed(range(digit_count)):
        shifted = passed_along(partial_grad.astype(jnp.bfloat16), "blk", -(1 << level)).astype(
            partial_grad.dtype
        )
        partial_grad = jnp.where(rep_index // (1 << level) % 2 == 1, shifted, partial_grad)
    grad_hw = lax.psum_scatter(
        partial_grad.astype(jnp.bfloat16), "rep", scatter_dimension=0, tiled=True
    )
    grad_feats = lax.dot_general(
        grad_hw, weight, (((1,), (1,)), ((), ())), preferred_element_type=jnp.float32
    ).astype(jnp.bfloat16)
    weight_terms = lax.dot_general(
        feats, grad_hw, (((0,), (0,)), ((), ())), preferred_element_type=jnp.float32
    )
    weight_part = lax.psum_scatter(
        weight_terms.astype(jnp.bfloat16), "rep", scatter_dimension=0, tiled=True
    ).astype(jnp.float32)
    group_bias = jnp.sum(grad_block.astype(jnp.float32), axis=0)
    grad_weight, grad_bias = lax.psum((weight_part, group_bias), "blk")
    return (out, grad_feats, grad_weight, grad_bias)


def solution(mesh):
    in_specs = (
        P(("blk", "rep"), None),
        P(),
        P(),
        P(("blk", "rep"), None),
        P("blk", "rep", None, None, None, None),
        P("blk", "rep", None, None),
        P("blk", "rep", None, None),
        P("blk", "rep", None),
    )
    out_specs = (P(("blk", "rep"), None), P(("blk", "rep"), None), P("rep", None), P())
    return jax.shard_map(body, mesh=mesh, in_specs=in_specs, out_specs=out_specs, check_vma=False)
```

profile of v0, /device:TPU:0, one launch (start us, length us, event | category | flops | bytes accessed | tf_op | source)
XLA Modules:
  0.0 1208.1 jit_solution(8378998526724302546)
XLA Ops:
  8.1 1.1 convolution_convert_fusion.2
  9.2 8.6 all_gather.6
  17.8 1.5 collective-permute-start
  19.3 15.5 %collective-permute-done = bf16[1024,256]{1,0:T(8,128)(2,1)S(1)} collective-permute-done((bf16[1024,256]{1,0:T(8,128)(2,1)S(1)}, bf16[1024,256]{1,0:T(8,128)(2,1)S(1)}, u32[]{:S(2)}, u32[]{:S(2)}) %collective-permute-start) | collective-permute-done | bytes 524320 | tf_op jit(solution)/shard_map/ppermute | solution.py:9
  35.0 4.0 slice_bitcast_fusion
  39.0 11.2 collective-permute-done.1
  51.7 219.8 %while.40 = (s32[]{:T(128)}, f32[1024,256]{1,0:T(8,128)S(1)}, s32[]{:T(128)}, s32[64]{0:T(128)S(1)}, bf16[64,128,128]{2,1,0:T(8,128)(2,1)S(1)}, /*index=5*/s32[6...) while((s32[]{:T(128)}, f32[1024,256]{1,0:T(8,128)S(1)}, ...), condition=%wide.region_1.2_spmd, body=%wide.region_0.1_spmd.sunk | while | flops 8421389 | bytes 360727 | solution.py:24
  271.5 259.8 %while.41 = (s32[]{:T(128)}, f32[1024,256]{1,0:T(8,128)S(1)}, s32[]{:T(128)}, s32[64]{0:T(128)S(1)}, bf16[64,128,128]{2,1,0:T(8,128)(2,1)}, /*index=5*/s32[64]{0...) while((s32[]{:T(128)}, f32[1024,256]{1,0:T(8,128)S(1)}, ...), condition=%wide.region_3.4_spmd, body=%wide.region_2.3_spmd.sunk | while | flops 8421389 | bytes 360727 | solution.py:24
  274.9 1.0 fusion.46
  279.1 1.0 fusion.46
  283.3 1.0 fusion.46
  287.4 1.0 fusion.46
  291.6 1.0 fusion.46
  295.8 1.0 fusion.46
  300.0 1.0 fusion.46
  304.1 1.0 fusion.46
  308.3 1.0 fusion.46
  312.5 1.0 fusion.46
  316.7 1.0 fusion.46
  320.9 1.0 fusion.46
  325.0 1.0 fusion.46
  329.2 1.0 fusion.46
  333.4 1.0 fusion.46
  337.6 1.0 fusion.46
  341.7 1.0 fusion.46
  345.9 1.0 fusion.46
  350.1 1.0 fusion.46
  354.3 1.0 fusion.46
  358.4 1.0 fusion.46
  366.8 1.0 fusion.46
  371.0 1.0 fusion.46
  375.1 1.0 fusion.46
  379.3 1.0 fusion.46
  383.5 1.0 fusion.46
  408.6 1.0 fusion.46
  412.7 1.0 fusion.46
  416.9 1.0 fusion.46
  421.1 1.0 fusion.46
  425.3 1.0 fusion.46
  446.2 1.0 fusion.46
  450.3 1.0 fusion.46
  454.5 1.0 fusion.46
  458.7 1.0 fusion.46
  462.9 1.0 fusion.46
  487.9 1.0 fusion.46
  492.1 1.0 fusion.46
  496.3 1.0 fusion.46
  500.5 1.0 fusion.46
  504.6 1.0 fusion.46
  525.5 1.0 fusion.46
  529.7 1.0 fusion.46
  532.3 43.0 %reduce-scatter.6.cloned.1.call-done = bf16[256,256]{1,0:T(8,128)(2,1)} async-done(((bf16[1024,256]{1,0:T(8,128)(2,1)}), bf16[256,256]{1,0:T(8,128)(2,1)}) %reduce-scatter.6.cloned.1.call-update) | async-done | bytes 131088 | tf_op jit(solution)/shard_map/reduce_scatter | solution.py:82
  575.3 1.7 multiply_convert_fusion
  577.0 6.8 all_gather.7
  583.8 256.2 %while.42 = (s32[]{:T(128)}, f32[1024,256]{1,0:T(8,128)S(1)}, s32[]{:T(128)}, s32[64]{0:T(128)S(1)}, bf16[64,128,128]{2,1,0:T(8,128)(2,1)}, /*index=5*/s32[64]{0...) while((s32[]{:T(128)}, f32[1024,256]{1,0:T(8,128)S(1)}, ...), condition=%wide.region_6.7_spmd, body=%wide.region_5.6_spmd.sunk | while | flops 8421389 | bytes 360727 | solution.py:42
  840.2 10.1 collective-permute-done.3
  850.3 217.9 %while.43 = (s32[]{:T(128)}, f32[1024,256]{1,0:T(8,128)S(1)}, s32[]{:T(128)}, s32[64]{0:T(128)S(1)}, bf16[64,128,128]{2,1,0:T(8,128)(2,1)}, /*index=5*/s32[64]{0...) while((s32[]{:T(128)}, f32[1024,256]{1,0:T(8,128)S(1)}, ...), condition=%wide.region_8.9_spmd, body=%wide.region_7.8_spmd.sunk | while | flops 8421389 | bytes 360727 | solution.py:42
  1068.3 9.2 collective-permute-done.4
  1077.7 10.0 collective-permute-done.5
  1088.6 50.4 %reduce-scatter.8.cloned.1.call-done = bf16[256,256]{1,0:T(8,128)(2,1)} async-done(((bf16[1024,256]{1,0:T(8,128)(2,1)}), bf16[256,256]{1,0:T(8,128)(2,1)}) %reduce-scatter.8.cloned.1.call-update) | async-done | bytes 131088 | tf_op jit(solution)/shard_map/reduce_scatter | solution.py:107
  1139.0 1.1 fusion.20
  1141.1 1.8 convolution_convert_fusion.1
  1142.9 18.2 %reduce-scatter.10.cloned.1.call-done = bf16[64,256]{1,0:T(8,128)(2,1)} async-done(((bf16[256,256]{1,0:T(8,128)(2,1)}), bf16[64,256]{1,0:T(8,128)(2,1)}) %reduce-scatter.10.cloned.1.call-update) | async-done | bytes 32784
  1161.9 38.9 %all-reduce.2 = (f32[64,256]{0,1:T(8,128)S(1)}, f32[256]{0:T(256)}) all-reduce(bf16[64,256]{0,1:T(8,128)(2,1)S(1)} %copy.15, f32[256]{0:T(256)S(1)} %convert_reduce_fusion), channel_id=1, replica_groups=mesh['blk'=8,'rep'=4] {'blk'}, use_global_device_ids=true, to_apply=%region_11.12 | all-reduce | flops 16640 | bytes 100352 | tf_op jit(solution)/shard_map/psum | solution.py:120
  (691 shorter events, 460.3 us)
Async XLA Ops:
  7.2 0.9 copy-start
  7.2 27.7 %copy-start.7 = (s32[1,1,2,64]{3,2,1,0:T(2,128)S(1)}, s32[1,1,2,64]{3,2,1,0:T(2,128)}, u32[]{:S(2)}) copy-start(s32[1,1,2,64]{3,2,1,0:T(2,128)} %param.21) | copy-start | bytes 1540
  7.2 27.7 %copy-start.6 = (s32[1,1,2,64]{3,2,1,0:T(2,128)S(1)}, s32[1,1,2,64]{3,2,1,0:T(2,128)}, u32[]{:S(2)}) copy-start(s32[1,1,2,64]{3,2,1,0:T(2,128)} %param.22) | copy-start | bytes 1540
  7.2 568.1 %reduce-scatter.6.cloned.1.call-start = ((), (), s32[]{:S(2)}) async-start(), calls=%async_computation.3 | async-start | bytes 655360 | tf_op jit(solution)/shard_map/reduce_scatter | solution.py:82
  17.8 17.0 %collective-permute-start = (bf16[1024,256]{1,0:T(8,128)(2,1)S(1)}, bf16[1024,256]{1,0:T(8,128)(2,1)S(1)}, u32[]{:S(2)}, u32[]{:S(2)}) collective-permute-start(bf16[1024,256]{1,0:T(8,128)(2,1)S(1)} %all_gather.6), channel_id=1, source_target_pairs={{0,4},{4,8},{8,12},{12,16},{16,20},{20,24},{24,28},{28,0},{1,5},{5... | collective-permute-start | bytes 1572872 | tf_op jit(solution)/shard_map/ppermute | solution.py:9
  34.8 15.4 %collective-permute-start.1 = (bf16[1024,256]{1,0:T(8,128)(2,1)S(1)}, bf16[1024,256]{1,0:T(8,128)(2,1)S(1)}, u32[]{:S(2)}, u32[]{:S(2)}) collective-permute-start(bf16[1024,256]{1,0:T(8,128)(2,1)S(1)} %broadcast_select_fusion), channel_id=1, source_target_pairs={{0,8},{4,12},{8,16},{12,20},{16,24},{20,28},{24,0},{28,4},{1,9},{5... | collective-permute-start | bytes 1572872 | tf_op jit(solution)/shard_map/ppermute | solution.py:9
  34.9 16.1 %copy-start.4 = (s32[1,1,2]{2,1,0:T(1,128)S(1)}, s32[1,1,2]{2,1,0:T(1,128)}, u32[]{:S(2)}) copy-start(s32[1,1,2]{2,1,0:T(1,128)} %param.23) | copy-start | bytes 28
  51.0 220.4 %collective-permute-start.2 = (bf16[1024,256]{1,0:T(8,128)(2,1)}, bf16[1024,256]{1,0:T(8,128)(2,1)}, u32[]{:S(2)}, u32[]{:S(2)}) collective-permute-start(bf16[1024,256]{1,0:T(8,128)(2,1)} %broadcast_select_fusion.1), channel_id=1, source_target_pairs={{0,16},{4,20},{8,24},{12,28},{16,0},{20,4},{24,8},{28,12},{1,17},{... | collective-permute-start | bytes 1572872 | tf_op jit(solution)/shard_map/ppermute | solution.py:9
  271.5 260.8 %copy-start.1 = (bf16[64,128,128]{2,1,0:T(8,128)(2,1)}, bf16[64,128,128]{2,1,0:T(8,128)(2,1)S(1)}, u32[]{:S(2)}) copy-start(bf16[64,128,128]{2,1,0:T(8,128)(2,1)S(1)} %get-tuple-element.563) | copy-start | bytes 6291460
  271.5 303.8 %copy-start.3 = (bf16[256,256]{1,0:T(8,128)(2,1)S(1)}, bf16[256,256]{1,0:T(8,128)(2,1)}, u32[]{:S(2)}) copy-start(bf16[256,256]{1,0:T(8,128)(2,1)} %param.19) | copy-start | bytes 393220
  271.5 303.8 %copy-start.5 = (f32[256]{0:T(256)S(1)}, f32[256]{0:T(256)}, u32[]{:S(2)}) copy-start(f32[256]{0:T(256)} %param.18) | copy-start | bytes 3076
  532.3 606.8 %reduce-scatter.8.cloned.1.call-start = ((), (), s32[]{:S(2)}) async-start(), calls=%async_computation.4 | async-start | bytes 655360 | tf_op jit(solution)/shard_map/reduce_scatter | solution.py:107
  840.1 10.1 collective-permute-start.3
  1068.2 9.2 collective-permute-start.4
  1077.6 63.5 %copy-start.2 = (bf16[256,256]{1,0:T(8,128)(2,1)S(1)}, bf16[256,256]{1,0:T(8,128)(2,1)}, u32[]{:S(2)}) copy-start(bf16[256,256]{1,0:T(8,128)(2,1)} %param.17) | copy-start | bytes 393220
  1077.6 10.0 collective-permute-start.5
  1088.6 72.5 %reduce-scatter.10.cloned.1.call-start = ((), (), s32[]{:S(2)}) async-start(), calls=%async_computation.5 | async-start | bytes 163840
Sparse Core Ops, SparseCore 0:
  532.4 42.8 reduce-scatter.5
  1088.7 50.2 reduce-scatter.7
  1141.4 19.5 reduce-scatter.9
where the time goes:
time: 1220 us; the launch traced here: 1210 us
  loops' own time  457 us (37%)
  local copies, waits for them, and re-layouts  278 us (23%)
  matrix products  230 us (19%)
  waiting for transfers between devices  167 us (14%)
  blocking collectives  54.3 us (4%)
  between operations  14 us (1%)
    another operation x2, loops' own time, forward_tiles(): return lax.fori_loop(0, live, forward_one_tile, total)  229 us
    another operation x2, loops' own time, backward_tiles(): return lax.fori_loop(0, live, backward_one_tile, total)  228 us
    dot_general x115, matrix products, forward_one_tile(): jnp.dot(tile_vals[position], source_rows, preferred_element_type=jnp.floa...  116 us
    dot_general x115, matrix products, backward_one_tile(): lax.dot_general(tile_vals[position], grad_rows, (((0,), (0,)), ((), ())),...  110 us
    dynamic_slice x115, local copies, waits for them, and re-layouts, forward_one_tile(): row_start = tile_row[position] * tile_size  67.7 us
    dynamic_slice x115, local copies, waits for them, and re-layouts, backward_one_tile(): col_start = tile_col[position] * tile_size  67.7 us
    dynamic_slice x115, local copies, waits for them, and re-layouts, backward_one_tile(): row_start = tile_row[position] * tile_size  67.5 us
    dynamic_slice x115, local copies, waits for them, and re-layouts, forward_one_tile(): col_start = tile_col[position] * tile_size  67.5 us
  transfers between devices with their start and end apart: 9, of which 8 were waited for; matrix products, arithmetic and copies ran while one was open for 10% of the time, Pallas kernels for 0%

commit v1 on v0

v1 whole, which is shorter than its diff:
```python
import functools

import jax
import jax.numpy as jnp
from jax import lax
from jax.experimental import pallas as pl
from jax.experimental.pallas import tpu as pltpu
from jax.sharding import PartitionSpec as P

MESH = pl.DeviceIdType.MESH
UNIT = 256
CHUNK = 16
HALF = 128


def remote(src, dst, send, recv, blk, rep):
    return pltpu.make_async_remote_copy(
        src_ref=src, dst_ref=dst, send_sem=send, recv_sem=recv, device_id=(blk, rep), device_id_type=MESH
    )


def layer_kernel(
    n_blk, n_rep, n_slot, tile, cells, tiles_side,
    inv_ref, feats_ref, weight_ref, bias_ref, gout_ref, tiles_hbm,
    out_ref, gf_ref, gw_ref, gb_ref,
    tiles, dense, hw, hwbuf, acc, part, aggbuf, gbuf, g_t, pbuf, ghbuf, feats_t,
    bias_mine, bias_buf, terms, wbuf, wsum, fin,
    tile_sem, hw_send, hw_recv, rs_send, rs_recv, ag_send, ag_recv, bw_send, bw_recv,
    bias_send, bias_recv, w_send, w_recv, fin_send, fin_recv,
):
    n_dev = n_blk * n_rep
    rows = feats_ref.shape[0]
    units = rows * n_rep // UNIT
    per = UNIT // rows
    width = feats_ref.shape[1]
    w_rows = width // n_rep
    owners = (w_rows // CHUNK) * (width // HALF)
    halves = width // HALF
    me_b = lax.axis_index("blk")
    me_r = lax.axis_index("rep")
    me = me_b * n_rep + me_r

    barrier = pltpu.get_barrier_semaphore()

    def greet(d, carry):
        other = lax.rem(me + d, n_dev)
        pl.semaphore_signal(
            barrier, inc=1, device_id=(other // n_rep, lax.rem(other, n_rep)), device_id_type=MESH
        )
        return carry

    lax.fori_loop(1, n_dev, greet, 0)

    loads = []
    for k in range(n_slot):
        span = pl.ds(k * cells, cells)
        load = pltpu.make_async_copy(tiles_hbm.at[span], tiles.at[span], tile_sem.at[k])
        load.start()
        loads.append(load)
    hw[...] = jnp.dot(
        feats_ref[...], weight_ref[...], preferred_element_type=jnp.float32
    ).astype(jnp.bfloat16)
    pl.semaphore_wait(barrier, n_dev - 1)

    def hw_copy(k, r):
        to = lax.rem(me_b + r + n_rep * k, n_blk)
        return remote(hw, hwbuf.at[k, me_r], hw_send.at[k, r], hw_recv.at[k, me_r], to, r)

    for k in range(n_slot):
        for r in range(n_rep):
            if k == 0 and r == 0:
                @pl.when(me_r != 0)
                def _():
                    hw_copy(0, 0).start()

                @pl.when(me_r == 0)
                def _():
                    hwbuf[0, 0] = hw[...]
            else:
                hw_copy(k, r).start()

    tiles[n_slot * cells] = jnp.zeros((tile, tile), jnp.bfloat16)
    for load in loads:
        load.wait()
    for k in range(n_slot):
        def fill(r, carry, k=k):
            for c in range(tiles_side):
                entry = inv_ref[k * tiles_side * tiles_side + r * tiles_side + c]
                dense[k, pl.ds(pl.multiple_of(r * tile, tile), tile), c * tile:(c + 1) * tile] = tiles[entry]
            return carry

        lax.fori_loop(0, tiles_side, fill, 0)
    feats_t[...] = feats_ref[...].T

    def hw_wait(k, src):
        remote(hw, hwbuf.at[k, src], hw_send.at[k, src], hw_recv.at[k, src], me_b, me_r).wait_recv()

    def rs_copy(j):
        return remote(part.at[j], aggbuf.at[me_r], rs_send.at[j], rs_recv.at[me_r], me_b, j)

    for k in range(n_slot):
        for u in range(units):
            for i in range(per):
                src = u * per + i
                if k == 0 and src == 0:
                    @pl.when(me_r != 0)
                    def _():
                        hw_wait(0, 0)
                else:
                    hw_wait(k, src)
            rhs = hwbuf[k, u * per:(u + 1) * per].reshape(UNIT, width)
            last = k == n_slot - 1 and u == units - 1
            for j in range(units):
                at = slice(j * UNIT, (j + 1) * UNIT)
                got = jnp.dot(
                    dense[k, at, u * UNIT:(u + 1) * UNIT], rhs, preferred_element_type=jnp.float32
                )
                if k + u > 0:
                    got = got + acc[at]
                acc[at] = got
                if last:
                    part[j * per:(j + 1) * per] = got.astype(jnp.bfloat16).reshape(per, rows, width)
                    for i in range(per):
                        @pl.when(me_r != j * per + i)
                        def _():
                            rs_copy(j * per + i).start()

    total = acc[pl.ds(pl.multiple_of(me_r * rows, rows), rows)]
    for d in range(1, n_rep):
        src = lax.rem(me_r + d, n_rep)
        remote(
            part.at[0], aggbuf.at[src], rs_send.at[src], rs_recv.at[src], me_b, src
        ).wait_recv()
        total = total + aggbuf[src].astype(jnp.float32)

    pre = total + bias_ref[...]
    logistic = jax.nn.sigmoid(pre)
    grad = (gout_ref[...].astype(jnp.float32) * logistic * (1.0 + pre * (1.0 - logistic))).astype(jnp.bfloat16)
    gbuf[me_r] = grad

    def ag_copy(d):
        to = lax.rem(me_r + d, n_rep)
        return remote(gbuf.at[me_r], gbuf.at[me_r], ag_send.at[d], ag_recv.at[me_r], me_b, to)

    for d in range(1, n_rep):
        ag_copy(d).start()
    out_ref[...] = (pre * logistic).astype(jnp.bfloat16)
    for d in range(1, n_rep):
        src = lax.rem(me_r + d, n_rep)
        remote(gbuf.at[src], gbuf.at[src], ag_send.at[d], ag_recv.at[src], me_b, src).wait_recv()
    for u in range(units):
        g_t[:, u * UNIT:(u + 1) * UNIT] = gbuf[u * per:(u + 1) * per].reshape(UNIT, width).T

    def bw_copy(k, j):
        to = lax.rem(me_b - me_r - n_rep * k + 2 * n_blk, n_blk)
        slot = k * n_rep + me_r
        return remote(pbuf.at[k, j], ghbuf.at[slot], bw_send.at[k, j], bw_recv.at[slot], to, j)

    for k in reversed(range(n_slot)):
        for u in range(units):
            term = jnp.dot(
                g_t[...], dense[k, :, u * UNIT:(u + 1) * UNIT], preferred_element_type=jnp.float32
            )
            pbuf[k, u * per:(u + 1) * per] = term.T.astype(jnp.bfloat16).reshape(per, rows, width)
            for i in range(per):
                j = u * per + i
                if k == 0 and j == 0:
                    @pl.when(me_r != 0)
                    def _():
                        bw_copy(0, 0).start()

                    @pl.when(me_r == 0)
                    def _():
                        ghbuf[0] = pbuf[0, 0]
                else:
                    bw_copy(k, j).start()

    bias_mine[...] = jnp.dot(
        jnp.ones((8, rows * n_rep), jnp.bfloat16),
        gbuf[...].reshape(rows * n_rep, width),
        preferred_element_type=jnp.float32,
    )

    def bias_send_one(d, carry):
        to = lax.rem(me_b + d, n_blk)
        remote(bias_mine, bias_buf.at[n_blk - 1 - d], bias_send, bias_recv, to, me_r).start()
        return carry

    lax.fori_loop(1, n_blk, bias_send_one, 0)

    total = jnp.zeros((rows, width), jnp.float32)
    for k in reversed(range(n_slot)):
        for r in range(n_rep):
            slot = k * n_rep + r

            def arrived():
                remote(
                    pbuf.at[0, 0], ghbuf.at[slot], bw_send.at[k, r], bw_recv.at[slot], me_b, me_r
                ).wait_recv()

            if slot == 0:
                pl.when(me_r != 0)(arrived)
            else:
                arrived()
            total = total + ghbuf[slot].astype(jnp.float32)
    gh = total.astype(jnp.bfloat16)
    w_terms = jnp.dot(feats_t[...], gh, preferred_element_type=jnp.float32).astype(jnp.bfloat16)
    for h in range(halves):
        terms[h] = w_terms[:, h * HALF:(h + 1) * HALF]

    def chunk_of(b, r):
        return terms.at[lax.rem(b, halves), pl.ds(pl.multiple_of(r * w_rows + b // halves * CHUNK, CHUNK), CHUNK)]

    def w_send_one(d, carry):
        other = lax.rem(me + d, n_dev)
        b, r = other // n_rep, lax.rem(other, n_rep)

        def go():
            remote(chunk_of(b, r), wbuf.at[n_dev - 1 - d], w_send, w_recv, b, r).start()

        if owners == n_blk:
            go()
        else:
            pl.when(b < owners)(go)
        return carry

    lax.fori_loop(1, n_dev, w_send_one, 0)
    gf_ref[...] = lax.dot_general(
        gh, weight_ref[...], (((1,), (1,)), ((), ())), preferred_element_type=jnp.float32
    ).astype(jnp.bfloat16)
    all_bias = bias_buf
    remote(all_bias, all_bias, bias_send, bias_recv, me_b, me_r).wait_recv()
    gb_ref[...] = (bias_mine[...] + jnp.sum(bias_buf[...], axis=0))[0:1]

    def fin_copy(d):
        to = lax.rem(me_b + d, n_blk)
        return remote(wsum, fin.at[me_b], fin_send.at[d], fin_recv.at[me_b], to, me_r)

    def own_chunk():
        remote(wbuf, wbuf, w_send, w_recv, me_b, me_r).wait_recv()
        mine = terms[
            lax.rem(me_b, halves), pl.ds(pl.multiple_of(me_r * w_rows + me_b // halves * CHUNK, CHUNK), CHUNK)
        ]
        wsum[...] = mine.astype(jnp.float32) + jnp.sum(wbuf[...].astype(jnp.float32), axis=0)
        for d in range(1, n_blk):
            fin_copy(d).start()
        fin[me_b] = wsum[...]

    if owners == n_blk:
        own_chunk()
    else:
        pl.when(me_b < owners)(own_chunk)
    for o in range(owners):
        @pl.when(me_b != o)
        def _():
            remote(wsum, fin.at[o], fin_send.at[0], fin_recv.at[o], me_b, me_r).wait_recv()

        at = o // halves * CHUNK
        gw_ref[at:at + CHUNK, (o % halves) * HALF:(o % halves + 1) * HALF] = fin[o]

    for k in range(n_slot):
        for r in range(n_rep):
            if k == 0 and r == 0:
                @pl.when(me_r != 0)
                def _():
                    hw_copy(0, 0).wait_send()
                    bw_copy(0, 0).wait_send()
            else:
                hw_copy(k, r).wait_send()
                bw_copy(k, r).wait_send()
    for j in range(n_rep):
        @pl.when(me_r != j)
        def _():
            rs_copy(j).wait_send()
    for d in range(1, n_rep):
        ag_copy(d).wait_send()
    remote(all_bias, all_bias, bias_send, bias_recv, me_b, me_r).wait_send()
    if owners == n_blk:
        remote(wbuf, wbuf, w_send, w_recv, me_b, me_r).wait_send()
    else:
        def w_left(d, carry):
            other = lax.rem(me + d, n_dev)

            @pl.when(other // n_rep < owners)
            def _():
                remote(wbuf.at[0], wbuf.at[0], w_send, w_recv, me_b, me_r).wait_send()
            return carry

        lax.fori_loop(1, n_dev, w_left, 0)

    def fin_left():
        for d in range(1, n_blk):
            fin_copy(d).wait_send()

    if owners == n_blk:
        fin_left()
    else:
        pl.when(me_b < owners)(fin_left)


def body(feats, weight, bias, grad_out, tile_values, tile_rows, tile_cols, tile_count):
    n_blk = lax.axis_size("blk")
    n_rep = lax.axis_size("rep")
    n_slot, cells, tile = tile_values.shape[2:5]
    rows, width = feats.shape
    n_dev = n_blk * n_rep
    part_rows = rows * n_rep
    side = part_rows // tile
    w_rows = width // n_rep
    owners = (w_rows // CHUNK) * (width // HALF)

    named = tile_rows[0, 0] * side + tile_cols[0, 0]
    live = jnp.arange(cells, dtype=jnp.int32)[None] < tile_count[0, 0][:, None]
    entry = jnp.arange(n_slot * cells, dtype=jnp.int32).reshape(n_slot, cells)
    hit = (named[:, None, :] == jnp.arange(side * side, dtype=jnp.int32)[None, :, None]) & live[:, None, :]
    inv = jnp.min(jnp.where(hit, entry[:, None, :], n_slot * cells), axis=2).reshape(-1)

    bf16, f32 = jnp.bfloat16, jnp.float32
    vmem = pl.BlockSpec(memory_space=pltpu.VMEM)
    dma = pltpu.SemaphoreType.DMA
    out, gf, gw, gb = pl.pallas_call(
        functools.partial(layer_kernel, n_blk, n_rep, n_slot, tile, cells, side),
        out_shape=(
            jax.ShapeDtypeStruct((rows, width), bf16),
            jax.ShapeDtypeStruct((rows, width), bf16),
            jax.ShapeDtypeStruct((w_rows, width), f32),
            jax.ShapeDtypeStruct((1, width), f32),
        ),
        in_specs=[pl.BlockSpec(memory_space=pltpu.SMEM), vmem, vmem, vmem, vmem, pl.BlockSpec(memory_space=pl.ANY)],
        out_specs=(vmem, vmem, vmem, vmem),
        scratch_shapes=[
            pltpu.VMEM((n_slot * cells + 1, tile, tile), bf16),
            pltpu.VMEM((n_slot, part_rows, part_rows), bf16),
            pltpu.VMEM((rows, width), bf16),
            pltpu.VMEM((n_slot, n_rep, rows, width), bf16),
            pltpu.VMEM((part_rows, width), f32),
            pltpu.VMEM((n_rep, rows, width), bf16),
            pltpu.VMEM((n_rep, rows, width), bf16),
            pltpu.VMEM((n_rep, rows, width), bf16),
            pltpu.VMEM((width, part_rows), bf16),
            pltpu.VMEM((n_slot, n_rep, rows, width), bf16),
            pltpu.VMEM((n_slot * n_rep, rows, width), bf16),
            pltpu.VMEM((width, rows), bf16),
            pltpu.VMEM((8, width), f32),
            pltpu.VMEM((n_blk - 1, 8, width), f32),
            pltpu.VMEM((width // HALF, width, HALF), bf16),
            pltpu.VMEM((n_dev - 1, CHUNK, HALF), bf16),
            pltpu.VMEM((CHUNK, HALF), f32),
            pltpu.VMEM((owners, CHUNK, HALF), f32),
            dma((n_slot,)),
            dma((n_slot, n_rep)),
            dma((n_slot, n_rep)),
            dma((n_rep,)),
            dma((n_rep,)),
            dma((n_rep,)),
            dma((n_rep,)),
            dma((n_slot, n_rep)),
            dma((n_slot * n_rep,)),
            dma,
            dma,
            dma,
            dma,
            dma((n_blk,)),
            dma((owners,)),
        ],
        compiler_params=pltpu.CompilerParams(
            collective_id=0, has_side_effects=True, vmem_limit_bytes=40 * 2 ** 20
        ),
        name="graph_layer",
    )(inv, feats, weight, bias.reshape(1, width), grad_out, tile_values.reshape(n_slot * cells, tile, tile))
    return (out, gf, gw, gb.reshape(width))


def solution(mesh):
    in_specs = (
        P(("blk", "rep"), None),
        P(),
        P(),
        P(("blk", "rep"), None),
        P("blk", "rep", None, None, None, None),
        P("blk", "rep", None, None),
        P("blk", "rep", None, None),
        P("blk", "rep", None),
    )
    out_specs = (P(("blk", "rep"), None), P(("blk", "rep"), None), P("rep", None), P())
    return jax.shard_map(body, mesh=mesh, in_specs=in_specs, out_specs=out_specs, check_vma=False)
```

time: 1220 us -> 95.7 us (0.08)
  loops' own time: 457 us -> 0 us
  local copies, waits for them, and re-layouts: 278 us -> 8.17 us
  matrix products: 230 us -> 0 us
  waiting for transfers between devices: 167 us -> 0 us
  Pallas kernels: 0 us -> 85.1 us
  blocking collectives: 54.3 us -> 0 us
  between operations: 14 us -> 0.65 us
    another operation x4 -> x0, loops' own time: 457 us -> none  [the longest x2 229 us: forward_tiles(): return lax.fori_loop(0, live, forward_one_tile, total)]
    dynamic_slice x460 -> x0, local copies, waits for them, and re-layouts: 270 us -> none  [the longest x115 67.7 us: forward_one_tile(): row_start = tile_row[position] * tile_size]
    dot_general x233 -> x0, matrix products: 230 us -> none  [the longest x115 116 us: forward_one_tile(): jnp.dot(tile_vals[position], source_rows, preferred_element_type=jnp.floa...]
    reduce_scatter x2 -> x0, waiting for transfers between devices: 93.3 us -> none  [the longest x1 50.4 us: body(): lax.psum_scatter(partial_grad.astype(jnp.bfloat16), 'rep', scatter_dimens...]
    pallas_call x0 -> x1, Pallas kernels: none -> 85.1 us  [body(): pl.pallas_call(functools.partial(layer_kernel, n_blk, n_rep, n_slot, tile...]
    ppermute x6 -> x0, waiting for transfers between devices: 55.9 us -> none  [passed_along(): lax.ppermute(x, axis, [(i, (i + by) % devices) for i in range(devices)])]
    psum x1 -> x0, blocking collectives: 38.9 us -> none  [body(): grad_weight, grad_bias = lax.psum((weight_part, group_bias), 'blk')]
    unnamed x4 -> x0, waiting for transfers between devices: 18.2 us -> none
  transfers between devices with their start and end apart: 9 -> 0, of which waited for: 8 -> 0; matrix products, arithmetic and copies ran while one was open for 10% -> 0% of each run, Pallas kernels for 0% -> 0%
where the time goes in v1:
time: 95.7 us; the launch traced here: 95.5 us
  Pallas kernels  85.1 us (89%)
  local copies, waits for them, and re-layouts  8.17 us (9%)
  other arithmetic  1.54 us (2%)
    pallas_call x1, Pallas kernels, body(): pl.pallas_call(functools.partial(layer_kernel, n_blk, n_rep, n_slot, tile...  85.1 us
    unnamed x14, local copies, waits for them, and re-layouts  8.09 us

profile of v1, /device:TPU:0, one launch (start us, length us, event | category | flops | bytes accessed | tf_op | source)
XLA Modules:
  0.0 95.5 jit_solution(7561636400619027240)
XLA Ops:
  0.6 0.7 iota_compare_fusion.1
  1.4 0.7 add_bitcast_fusion
  2.1 0.1 select_reduce_fusion
  2.2 0.1 reshape.66.inv_ref
  2.3 0.0 copy-start
  2.3 2.2 %copy-done = bf16[1,1,2,64,128,128]{5,4,3,2,1,0:T(8,128)(2,1)S(1)} copy-done((bf16[1,1,2,64,128,128]{5,4,3,2,1,0:T(8,128)(2,1)S(1)}, bf16[1,1,2,64,128,128]{5,4,3,2,1,0:T(8,128)(2,1)}, u32[]{:S(2)}) %copy-start) | copy-done | bytes 4194328
  4.5 0.0 copy-start.1
  4.5 0.9 copy-done.1
  5.4 0.0 copy-start.2
  5.4 0.9 copy-done.2
  6.3 0.0 copy-start.3
  6.3 0.9 copy-done.3
  7.2 0.0 copy-start.4
  7.2 0.7 copy-done.4
  7.9 85.1 %graph_layer.1 = (bf16[256,256]{1,0:T(8,128)(2,1)S(1)}, bf16[256,256]{1,0:T(8,128)(2,1)S(1)}, f32[64,256]{1,0:T(8,128)S(1)}, f32[1,256]{1,0:T(1,128)S(1)}) custom-call(s32[128]{0:T(128)S(1)} %reshape.66.inv_ref, bf16[256,256]{1,0:T(8,128)(2,1)S(1)} %copy-done.1, bf16[256,256]{1,0:T(8,128)(2,1)S(1)} %copy-done.2, f32[1,256]{1,0:T(1,128)S(1)} %bitcast.8, ...), custom_call_target="tpu_custom_call" | custom-call | tf_op jit(solution)/shard_map/graph_layer/pallas_call | solution.py:321
  93.0 0.7 copy.16
  93.6 0.7 copy.17
  94.3 0.6 copy.18
  94.9 0.6 copy.19
  (1 shorter events, 0.0 us)
Async XLA Ops:
  2.3 2.2 %copy-start = (bf16[1,1,2,64,128,128]{5,4,3,2,1,0:T(8,128)(2,1)S(1)}, bf16[1,1,2,64,128,128]{5,4,3,2,1,0:T(8,128)(2,1)}, u32[]{:S(2)}) copy-start(bf16[1,1,2,64,128,128]{5,4,3,2,1,0:T(8,128)(2,1)} %param.12) | copy-start | bytes 12582916
  4.5 0.9 copy-start.1
  5.4 0.9 copy-start.2
  6.3 0.9 copy-start.3
  7.2 0.7 copy-start.4

commit v2 on v1

--- a/solution.py
+++ b/solution.py
@@ -21,11 +21,11 @@
 
 def layer_kernel(
     n_blk, n_rep, n_slot, tile, cells, tiles_side,
-    inv_ref, feats_ref, weight_ref, bias_ref, gout_ref, tiles_hbm,
+    inv_ref, feats_hbm, weight_hbm, bias_hbm, gout_hbm, tiles_hbm,
     out_ref, gf_ref, gw_ref, gb_ref,
-    tiles, dense, hw, hwbuf, acc, part, aggbuf, gbuf, g_t, pbuf, ghbuf, feats_t,
-    bias_mine, bias_buf, terms, wbuf, wsum, fin,
-    tile_sem, hw_send, hw_recv, rs_send, rs_recv, ag_send, ag_recv, bw_send, bw_recv,
+    feats_ref, weight_ref, bias_ref, gout_ref, tiles, dense, hw, hw_other, hwbuf, acc, part, aggbuf, gbuf, g_t, pbuf, ghbuf, feats_t,
+    cross, bias_mine, bias_buf, terms, wbuf, wsum, fin,
+    in_sem, tile_sem, swap_send, swap_recv, cross_send, cross_recv, hw_send, hw_recv, rs_send, rs_recv, ag_send, ag_recv, bw_send, bw_recv,
     bias_send, bias_recv, w_send, w_recv, fin_send, fin_recv,
 ):
     n_dev = n_blk * n_rep
@@ -39,7 +39,23 @@
     me_b = lax.axis_index("blk")
     me_r = lax.axis_index("rep")
     me = me_b * n_rep + me_r
-
+    half = me_b // n_rep
+    place = lax.rem(me_b, n_rep)
+    partner = lax.rem(me_b + n_rep, n_blk)
+    near_slot = jnp.where(place < me_r, 1, 0)
+
+    small = []
+    for i, (src, dst) in enumerate(
+        ((feats_hbm, feats_ref), (weight_hbm, weight_ref), (bias_hbm, bias_ref), (gout_hbm, gout_ref))
+    ):
+        small.append(pltpu.make_async_copy(src, dst, in_sem.at[i]))
+        small[-1].start()
+    loads = []
+    for k in range(n_slot):
+        span = pl.ds(k * cells, cells)
+        load = pltpu.make_async_copy(tiles_hbm.at[span], tiles.at[span], tile_sem.at[k])
+        load.start()
+        loads.append(load)
     barrier = pltpu.get_barrier_semaphore()
 
     def greet(d, carry):
@@ -51,45 +67,52 @@
 
     lax.fori_loop(1, n_dev, greet, 0)
 
-    loads = []
-    for k in range(n_slot):
-        span = pl.ds(k * cells, cells)
-        load = pltpu.make_async_copy(tiles_hbm.at[span], tiles.at[span], tile_sem.at[k])
-        load.start()
-        loads.append(load)
+    small[0].wait()
+    small[1].wait()
     hw[...] = jnp.dot(
         feats_ref[...], weight_ref[...], preferred_element_type=jnp.float32
     ).astype(jnp.bfloat16)
     pl.semaphore_wait(barrier, n_dev - 1)
 
-    def hw_copy(k, r):
-        to = lax.rem(me_b + r + n_rep * k, n_blk)
-        return remote(hw, hwbuf.at[k, me_r], hw_send.at[k, r], hw_recv.at[k, me_r], to, r)
-
-    for k in range(n_slot):
-        for r in range(n_rep):
-            if k == 0 and r == 0:
+    swap = remote(hw, hw_other, swap_send, swap_recv, partner, me_r)
+    swap.start()
+
+    def hw_copy(h, r):
+        to = half * n_rep + lax.rem(place + r, n_rep)
+        src = hw if h == 0 else hw_other
+        return remote(src, hwbuf.at[h, me_r], hw_send.at[h, r], hw_recv.at[h, me_r], to, r)
+
+    def hw_share(h):
+        for r in reversed(range(n_rep)):
+            if r == 0:
                 @pl.when(me_r != 0)
                 def _():
-                    hw_copy(0, 0).start()
+                    hw_copy(h, 0).start()
 
                 @pl.when(me_r == 0)
                 def _():
-                    hwbuf[0, 0] = hw[...]
+                    hwbuf[h, 0] = hw[...] if h == 0 else hw_other[...]
             else:
-                hw_copy(k, r).start()
+                hw_copy(h, r).start()
+
+    hw_share(0)
 
     tiles[n_slot * cells] = jnp.zeros((tile, tile), jnp.bfloat16)
     for load in loads:
         load.wait()
-    for k in range(n_slot):
-        def fill(r, carry, k=k):
+    for h in range(2):
+        base = jnp.where(near_slot == 1, 1 - h, h) * tiles_side * tiles_side
+
+        def fill(r, carry, h=h, base=base):
             for c in range(tiles_side):
-                entry = inv_ref[k * tiles_side * tiles_side + r * tiles_side + c]
-                dense[k, pl.ds(pl.multiple_of(r * tile, tile), tile), c * tile:(c + 1) * tile] = tiles[entry]
+                entry = inv_ref[base + r * tiles_side + c]
+                dense[h, pl.ds(pl.multiple_of(r * tile, tile), tile), c * tile:(c + 1) * tile] = tiles[entry]
             return carry
 
         lax.fori_loop(0, tiles_side, fill, 0)
+        if h == 0:
+            swap.wait_recv()
+            hw_share(1)
     feats_t[...] = feats_ref[...].T
 
     def hw_wait(k, src):
@@ -102,10 +125,10 @@
         for u in range(units):
             for i in range(per):
                 src = u * per + i
-                if k == 0 and src == 0:
+                if src == 0:
                     @pl.when(me_r != 0)
                     def _():
-                        hw_wait(0, 0)
+                        hw_wait(k, 0)
                 else:
                     hw_wait(k, src)
             rhs = hwbuf[k, u * per:(u + 1) * per].reshape(UNIT, width)
@@ -133,6 +156,8 @@
         ).wait_recv()
         total = total + aggbuf[src].astype(jnp.float32)
 
+    small[2].wait()
+    small[3].wait()
     pre = total + bias_ref[...]
     logistic = jax.nn.sigmoid(pre)
     grad = (gout_ref[...].astype(jnp.float32) * logistic * (1.0 + pre * (1.0 - logistic))).astype(jnp.bfloat16)
@@ -152,7 +177,7 @@
         g_t[:, u * UNIT:(u + 1) * UNIT] = gbuf[u * per:(u + 1) * per].reshape(UNIT, width).T
 
     def bw_copy(k, j):
-        to = lax.rem(me_b - me_r - n_rep * k + 2 * n_blk, n_blk)
+        to = half * n_rep + lax.rem(place - me_r + n_rep, n_rep)
         slot = k * n_rep + me_r
         return remote(pbuf.at[k, j], ghbuf.at[slot], bw_send.at[k, j], bw_recv.at[slot], to, j)
 
@@ -164,14 +189,14 @@
             pbuf[k, u * per:(u + 1) * per] = term.T.astype(jnp.bfloat16).reshape(per, rows, width)
             for i in range(per):
                 j = u * per + i
-                if k == 0 and j == 0:
+                if j == 0:
                     @pl.when(me_r != 0)
                     def _():
-                        bw_copy(0, 0).start()
+                        bw_copy(k, 0).start()
 
                     @pl.when(me_r == 0)
                     def _():
-                        ghbuf[0] = pbuf[0, 0]
+                        ghbuf[k * n_rep] = pbuf[k, 0]
                 else:
                     bw_copy(k, j).start()
 
@@ -188,21 +213,29 @@
 
     lax.fori_loop(1, n_blk, bias_send_one, 0)
 
-    total = jnp.zeros((rows, width), jnp.float32)
-    for k in reversed(range(n_slot)):
+    def summed(h):
+        total = jnp.zeros((rows, width), jnp.float32)
         for r in range(n_rep):
-            slot = k * n_rep + r
+            slot = h * n_rep + r
 
             def arrived():
                 remote(
-                    pbuf.at[0, 0], ghbuf.at[slot], bw_send.at[k, r], bw_recv.at[slot], me_b, me_r
+                    pbuf.at[0, 0], ghbuf.at[slot], bw_send.at[h, r], bw_recv.at[slot], me_b, me_r
                 ).wait_recv()
 
-            if slot == 0:
+            if r == 0:
                 pl.when(me_r != 0)(arrived)
             else:
                 arrived()
             total = total + ghbuf[slot].astype(jnp.float32)
+        return total
+
+    cross[...] = summed(1).astype(jnp.bfloat16)
+    over = remote(cross, ghbuf.at[2 * n_rep], cross_send, cross_recv, partner, me_r)
+    over.start()
+    total = summed(0)
+    over.wait_recv()
+    total = total + ghbuf[2 * n_rep].astype(jnp.float32)
     gh = total.astype(jnp.bfloat16)
     w_terms = jnp.dot(feats_t[...], gh, preferred_element_type=jnp.float32).astype(jnp.bfloat16)
     for h in range(halves):
@@ -258,13 +291,15 @@
         at = o // halves * CHUNK
         gw_ref[at:at + CHUNK, (o % halves) * HALF:(o % halves + 1) * HALF] = fin[o]
 
+    swap.wait_send()
+    over.wait_send()
     for k in range(n_slot):
         for r in range(n_rep):
-            if k == 0 and r == 0:
+            if r == 0:
                 @pl.when(me_r != 0)
                 def _():
-                    hw_copy(0, 0).wait_send()
-                    bw_copy(0, 0).wait_send()
+                    hw_copy(k, 0).wait_send()
+                    bw_copy(k, 0).wait_send()
             else:
                 hw_copy(k, r).wait_send()
                 bw_copy(k, r).wait_send()
@@ -315,6 +350,7 @@
     hit = (named[:, None, :] == jnp.arange(side * side, dtype=jnp.int32)[None, :, None]) & live[:, None, :]
     inv = jnp.min(jnp.where(hit, entry[:, None, :], n_slot * cells), axis=2).reshape(-1)
 
+    assert n_slot == 2 and n_blk == 2 * n_rep
     bf16, f32 = jnp.bfloat16, jnp.float32
     vmem = pl.BlockSpec(memory_space=pltpu.VMEM)
     dma = pltpu.SemaphoreType.DMA
@@ -326,11 +362,16 @@
             jax.ShapeDtypeStruct((w_rows, width), f32),
             jax.ShapeDtypeStruct((1, width), f32),
         ),
-        in_specs=[pl.BlockSpec(memory_space=pltpu.SMEM), vmem, vmem, vmem, vmem, pl.BlockSpec(memory_space=pl.ANY)],
+        in_specs=[pl.BlockSpec(memory_space=pltpu.SMEM)] + [pl.BlockSpec(memory_space=pl.ANY)] * 5,
         out_specs=(vmem, vmem, vmem, vmem),
         scratch_shapes=[
+            pltpu.VMEM((rows, width), bf16),
+            pltpu.VMEM((width, width), bf16),
+            pltpu.VMEM((1, width), f32),
+            pltpu.VMEM((rows, width), bf16),
             pltpu.VMEM((n_slot * cells + 1, tile, tile), bf16),
             pltpu.VMEM((n_slot, part_rows, part_rows), bf16),
+            pltpu.VMEM((rows, width), bf16),
             pltpu.VMEM((rows, width), bf16),
             pltpu.VMEM((n_slot, n_rep, rows, width), bf16),
             pltpu.VMEM((part_rows, width), f32),
@@ -339,15 +380,21 @@
             pltpu.VMEM((n_rep, rows, width), bf16),
             pltpu.VMEM((width, part_rows), bf16),
             pltpu.VMEM((n_slot, n_rep, rows, width), bf16),
-            pltpu.VMEM((n_slot * n_rep, rows, width), bf16),
+            pltpu.VMEM((n_slot * n_rep + 1, rows, width), bf16),
             pltpu.VMEM((width, rows), bf16),
+            pltpu.VMEM((rows, width), bf16),
             pltpu.VMEM((8, width), f32),
             pltpu.VMEM((n_blk - 1, 8, width), f32),
             pltpu.VMEM((width // HALF, width, HALF), bf16),
             pltpu.VMEM((n_dev - 1, CHUNK, HALF), bf16),
             pltpu.VMEM((CHUNK, HALF), f32),
             pltpu.VMEM((owners, CHUNK, HALF), f32),
+            dma((4,)),
             dma((n_slot,)),
+            dma,
+            dma,
+            dma,
+            dma,
             dma((n_slot, n_rep)),
             dma((n_slot, n_rep)),
             dma((n_rep,)),
@@ -364,7 +411,7 @@
             dma((owners,)),
         ],
         compiler_params=pltpu.CompilerParams(
-            collective_id=0, has_side_effects=True, vmem_limit_bytes=40 * 2 ** 20
+            collective_id=0, has_side_effects=True, vmem_limit_bytes=56 * 2 ** 20
         ),
         name="graph_layer",
     )(inv, feats, weight, bias.reshape(1, width), grad_out, tile_values.reshape(n_slot * cells, tile, tile))

time: 95.7 us -> 86 us (0.90)
  Pallas kernels: 85.1 us -> 77.2 us
  local copies, waits for them, and re-layouts: 8.17 us -> 6.44 us
    pallas_call x1, Pallas kernels: 85.1 us -> 77.2 us  [body(): pl.pallas_call(functools.partial(layer_kernel, n_blk, n_rep, n_slot, tile...]
    unnamed x14 -> x4, local copies, waits for them, and re-layouts: 8.09 us -> 5.84 us
where the time goes in v2:
time: 86 us; the launch traced here: 85.8 us
  Pallas kernels  77.2 us (90%)
  local copies, waits for them, and re-layouts  6.44 us (7%)
  other arithmetic  1.54 us (2%)
    pallas_call x1, Pallas kernels, body(): pl.pallas_call(functools.partial(layer_kernel, n_blk, n_rep, n_slot, tile...  77.2 us
    unnamed x4, local copies, waits for them, and re-layouts  5.84 us

profile of v2, /device:TPU:0, one launch (start us, length us, event | category | flops | bytes accessed | tf_op | source)
XLA Modules:
  0.0 85.8 jit_solution(13949076274908667402)
XLA Ops:
  0.6 0.7 iota_compare_fusion.1
  1.4 0.7 add_bitcast_fusion
  2.1 0.1 select_reduce_fusion
  2.2 0.6 reshape.66.inv_ref
  2.8 77.2 %graph_layer.1 = (bf16[256,256]{1,0:T(8,128)(2,1)}, bf16[256,256]{1,0:T(8,128)(2,1)}, f32[64,256]{1,0:T(8,128)}, f32[1,256]{1,0:T(1,128)}) custom-call(s32[128]{0:T(128)} %reshape.66.inv_ref, bf16[256,256]{1,0:T(8,128)(2,1)} %feats_hbm.1, bf16[256,256]{1,0:T(8,128)(2,1)} %weight_hbm.1, f32[1,256]{1,0:T(1,128)} %bitcast.8, bf16[256,256]{1,0:T(8,128)(2,1)} %gout_hbm.1, ...), custom_call_target="tpu_custom_call" | custom-call | tf_op jit(solution)/shard_map/graph_layer/pallas_call | solution.py:357
  79.9 1.6 %copy.16 = bf16[256,256]{1,0:T(8,128)(2,1)} copy(bf16[256,256]{1,0:T(8,128)(2,1)} %get-tuple-element.16) | data formatting | bytes 262144
  81.5 1.6 %copy.17 = bf16[256,256]{1,0:T(8,128)(2,1)} copy(bf16[256,256]{1,0:T(8,128)(2,1)} %get-tuple-element.17) | data formatting | bytes 262144
  83.1 1.5 %copy.18 = f32[64,256]{1,0:T(8,128)} copy(f32[64,256]{1,0:T(8,128)} %get-tuple-element.18) | data formatting | bytes 131072
  84.6 1.2 %copy.19 = f32[256]{0:T(256)} copy(f32[256]{0:T(256)} %bitcast.7) | data formatting | bytes 2048
  (1 shorter events, 0.0 us)

commit v3 on v2

v3 whole, which is shorter than its diff:
```python
import functools

import jax
import jax.numpy as jnp
from jax import lax
from jax.experimental import pallas as pl
from jax.experimental.pallas import tpu as pltpu
from jax.sharding import PartitionSpec as P

MESH = pl.DeviceIdType.MESH
UNIT = 256
CHUNK = 16
HALF = 128


def remote(src, dst, send, recv, blk, rep):
    return pltpu.make_async_remote_copy(
        src_ref=src, dst_ref=dst, send_sem=send, recv_sem=recv, device_id=(blk, rep), device_id_type=MESH
    )


def layer_kernel(
    n_blk, n_rep, n_slot, tile, cells, tiles_side,
    inv_ref, feats_hbm, weight_hbm, bias_hbm, gout_hbm, tiles_hbm,
    out_hbm, gf_hbm, gw_hbm, gb_hbm,
    feats_ref, weight_ref, bias_ref, gout_ref, out_ref, gf_ref, gw_ref, gb_ref,
    tiles, dense, dense_t, hw, hw_other, hwbuf, acc, part, aggbuf, gbuf, pbuf, ghbuf, feats_t,
    cross, bias_mine, bias_buf, terms, wbuf, wsum, fin,
    in_sem, out_sem, tile_sem, swap_send, swap_recv, cross_send, cross_recv, hw_send, hw_recv,
    rs_send, rs_recv, ag_send, ag_recv, bw_send, bw_recv,
    bias_send, bias_recv, w_send, w_recv, fin_send, fin_recv,
):
    n_dev = n_blk * n_rep
    rows, width = feats_ref.shape
    units = rows * n_rep // UNIT
    per = UNIT // rows
    w_rows = width // n_rep
    halves = width // HALF
    groups = w_rows // CHUNK
    owners = groups * halves
    f32, bf16 = jnp.float32, jnp.bfloat16
    me_b = lax.axis_index("blk")
    me_r = lax.axis_index("rep")
    me = me_b * n_rep + me_r
    half = me_b // n_rep
    place = lax.rem(me_b, n_rep)
    partner = lax.rem(me_b + n_rep, n_blk)
    near_slot = jnp.where(place < me_r, 1, 0)

    def columns(c):
        return slice(c * HALF, (c + 1) * HALF)

    def unless(i, task):
        if i == 0:
            pl.when(me_r != 0)(task)
        else:
            task()

    small = []
    for i, (src, dst) in enumerate(
        ((feats_hbm, feats_ref), (weight_hbm, weight_ref), (bias_hbm, bias_ref), (gout_hbm, gout_ref))
    ):
        small.append(pltpu.make_async_copy(src, dst, in_sem.at[i]))
        small[-1].start()
    loads = []
    for k in range(n_slot):
        span = pl.ds(k * cells, cells)
        load = pltpu.make_async_copy(tiles_hbm.at[span], tiles.at[span], tile_sem.at[k])
        load.start()
        loads.append(load)
    barrier = pltpu.get_barrier_semaphore()

    def greet(d, carry):
        other = lax.rem(me + d, n_dev)
        pl.semaphore_signal(
            barrier, inc=1, device_id=(other // n_rep, lax.rem(other, n_rep)), device_id_type=MESH
        )
        return carry

    lax.fori_loop(1, n_dev, greet, 0)

    small[0].wait()
    small[1].wait()
    first = jnp.dot(feats_ref[...], weight_ref[...], preferred_element_type=f32).astype(bf16)
    for c in range(halves):
        hw[c] = first[:, columns(c)]
    pl.semaphore_wait(barrier, n_dev - 1)

    swaps = [
        remote(hw.at[c], hw_other.at[c], swap_send.at[c], swap_recv.at[c], partner, me_r) for c in range(halves)
    ]

    def hw_copy(c, h, r):
        to = half * n_rep + lax.rem(place + r, n_rep)
        src = hw if h == 0 else hw_other
        return remote(src.at[c], hwbuf.at[c, h, me_r], hw_send.at[c, h, r], hw_recv.at[c, h, me_r], to, r)

    def hw_share(c, h):
        for r in reversed(range(n_rep)):
            unless(r, lambda: hw_copy(c, h, r).start())

        @pl.when(me_r == 0)
        def _():
            hwbuf[c, h, 0] = hw[c] if h == 0 else hw_other[c]

    def fill(h):
        base = jnp.where(near_slot == 1, 1 - h, h) * tiles_side * tiles_side

        def fill_rows(r, carry):
            at = pl.ds(pl.multiple_of(r * tile, tile), tile)
            for c in range(tiles_side):
                dense[h, at, c * tile:(c + 1) * tile] = tiles[inv_ref[base + r * tiles_side + c]]
            return carry

        lax.fori_loop(0, tiles_side, fill_rows, 0)

    def fill_transposed(h):
        base = jnp.where(near_slot == 1, 1 - h, h) * tiles_side * tiles_side

        def fill_rows(c, carry):
            at = pl.ds(pl.multiple_of(c * tile, tile), tile)
            for r in range(tiles_side):
                dense_t[h, at, r * tile:(r + 1) * tile] = tiles[inv_ref[base + r * tiles_side + c]].T
            return carry

        lax.fori_loop(0, tiles_side, fill_rows, 0)

    for c in range(halves):
        swaps[c].start()
        if c == 0:
            hw_share(0, 0)
    tiles[n_slot * cells] = jnp.zeros((tile, tile), bf16)
    for load in loads:
        load.wait()
    fill(0)
    swaps[0].wait_recv()
    hw_share(0, 1)
    for c in range(1, halves):
        hw_share(c, 0)
    fill(1)
    for c in range(1, halves):
        swaps[c].wait_recv()
        hw_share(c, 1)
    fill_transposed(1)
    fill_transposed(0)
    feats_t[...] = feats_ref[...].T

    def hw_wait(c, h, src):
        remote(
            hw.at[c], hwbuf.at[c, h, src], hw_send.at[c, h, src], hw_recv.at[c, h, src], me_b, me_r
        ).wait_recv()

    def rs_copy(c, j):
        return remote(part.at[c, j], aggbuf.at[c, me_r], rs_send.at[c, j], rs_recv.at[c, me_r], me_b, j)

    def forward(c):
        for h in range(2):
            for u in range(units):
                for src in range(u * per, (u + 1) * per):
                    unless(src, lambda: hw_wait(c, h, src))
                rhs = hwbuf[c, h, u * per:(u + 1) * per].reshape(UNIT, HALF)
                last = h == 1 and u == units - 1
                for j in range(units):
                    at = slice(j * UNIT, (j + 1) * UNIT)
                    got = jnp.dot(dense[h, at, u * UNIT:(u + 1) * UNIT], rhs, preferred_element_type=f32)
                    if h + u > 0:
                        got = got + acc[c, at]
                    acc[c, at] = got
                    if last:
                        part[c, j * per:(j + 1) * per] = got.astype(bf16).reshape(per, rows, HALF)
                        for i in range(j * per, (j + 1) * per):
                            pl.when(me_r != i)(lambda: rs_copy(c, i).start())

    def ag_copy(c, d):
        to = lax.rem(me_r + d, n_rep)
        return remote(
            gbuf.at[c, me_r], gbuf.at[c, me_r], ag_send.at[c, d], ag_recv.at[c, me_r], me_b, to
        )

    def activate(c):
        total = acc[c, pl.ds(pl.multiple_of(me_r * rows, rows), rows)]
        for d in range(1, n_rep):
            src = lax.rem(me_r + d, n_rep)
            remote(
                part.at[c, 0], aggbuf.at[c, src], rs_send.at[c, src], rs_recv.at[c, src], me_b, src
            ).wait_recv()
            total = total + aggbuf[c, src].astype(f32)
        pre = total + bias_ref[:, columns(c)]
        logistic = jax.nn.sigmoid(pre)
        cotangent = gout_ref[:, columns(c)].astype(f32)
        gbuf[c, me_r] = (cotangent * logistic * (1.0 + pre * (1.0 - logistic))).astype(bf16)
        for d in range(1, n_rep):
            ag_copy(c, d).start()
        out_ref[:, columns(c)] = (pre * logistic).astype(bf16)

    def bw_copy(c, h, j):
        to = half * n_rep + lax.rem(place - me_r + n_rep, n_rep)
        slot = h * n_rep + me_r
        return remote(pbuf.at[c, h, j], ghbuf.at[c, slot], bw_send.at[c, h, j], bw_recv.at[c, slot], to, j)

    def backward(c):
        for d in range(1, n_rep):
            src = lax.rem(me_r + d, n_rep)
            remote(
                gbuf.at[c, src], gbuf.at[c, src], ag_send.at[c, d], ag_recv.at[c, src], me_b, src
            ).wait_recv()
        grads = gbuf[c].reshape(rows * n_rep, HALF)
        for h in (1, 0):
            for u in range(units):
                term = jnp.dot(dense_t[h, u * UNIT:(u + 1) * UNIT], grads, preferred_element_type=f32)
                pbuf[c, h, u * per:(u + 1) * per] = term.astype(bf16).reshape(per, rows, HALF)
                for j in range(u * per, (u + 1) * per):
                    unless(j, lambda: bw_copy(c, h, j).start())
                    if j == 0:
                        @pl.when(me_r == 0)
                        def _():
                            ghbuf[c, h * n_rep] = pbuf[c, h, 0]
        bias_mine[:, columns(c)] = jnp.dot(
            jnp.ones((8, rows * n_rep), bf16), grads, preferred_element_type=f32
        )

    def arrived(c, slot):
        remote(
            pbuf.at[c, 0, 0], ghbuf.at[c, slot], bw_send.at[c, 0, 0], bw_recv.at[c, slot], me_b, me_r
        ).wait_recv()

    def summed(c, h):
        total = jnp.zeros((rows, HALF), f32)
        for r in range(n_rep):
            unless(r, lambda: arrived(c, h * n_rep + r))
            total = total + ghbuf[c, h * n_rep + r].astype(f32)
        return total

    overs = [
        remote(cross.at[c], ghbuf.at[c, 2 * n_rep], cross_send.at[c], cross_recv.at[c], partner, me_r)
        for c in range(halves)
    ]

    def send_over(c):
        cross[c] = summed(c, 1).astype(bf16)
        overs[c].start()

    def w_copy(c, g, r):
        to = (g * halves + c) * n_rep + r
        slot = lax.rem(me - to + n_dev, n_dev) - 1
        at = r * w_rows + g * CHUNK
        return remote(
            terms.at[c, at:at + CHUNK], wbuf.at[slot], w_send, w_recv, g * halves + c, r
        )

    def owned(c):
        total = summed(c, 0)
        overs[c].wait_recv()
        gh = (total + ghbuf[c, 2 * n_rep].astype(f32)).astype(bf16)
        terms[c] = jnp.dot(feats_t[...], gh, preferred_element_type=f32).astype(bf16)
        for g in range(groups):
            for r in range(n_rep):
                pl.when(me != (g * halves + c) * n_rep + r)(lambda: w_copy(c, g, r).start())
        return lax.dot_general(
            gh, weight_ref[:, columns(c)], (((1,), (1,)), ((), ())), preferred_element_type=f32
        )

    for c in range(halves):
        forward(c)
    small[2].wait()
    small[3].wait()
    for c in range(halves):
        activate(c)
    results = [
        pltpu.make_async_copy(src, dst, out_sem.at[i])
        for i, (src, dst) in enumerate(
            ((out_ref, out_hbm), (gf_ref, gf_hbm), (gw_ref, gw_hbm), (gb_ref, gb_hbm))
        )
    ]
    results[0].start()
    for c in range(halves):
        backward(c)

    def bias_send_one(d, carry):
        to = lax.rem(me_b + d, n_blk)
        remote(bias_mine, bias_buf.at[n_blk - 1 - d], bias_send, bias_recv, to, me_r).start()
        return carry

    lax.fori_loop(1, n_blk, bias_send_one, 0)

    for c in range(halves):
        send_over(c)
    feat_grad = owned(0)
    for c in range(1, halves):
        feat_grad = feat_grad + owned(c)
    gf_ref[...] = feat_grad.astype(bf16)
    results[1].start()
    remote(bias_buf, bias_buf, bias_send, bias_recv, me_b, me_r).wait_recv()
    gb_ref[...] = (bias_mine[...] + jnp.sum(bias_buf[...], axis=0))[0:1]
    results[3].start()

    def fin_copy(d):
        to = lax.rem(me_b + d, n_blk)
        return remote(wsum, fin.at[me_b], fin_send.at[d], fin_recv.at[me_b], to, me_r)

    def own_chunk():
        remote(wbuf, wbuf, w_send, w_recv, me_b, me_r).wait_recv()
        mine = terms[
            lax.rem(me_b, halves), pl.ds(pl.multiple_of(me_r * w_rows + me_b // halves * CHUNK, CHUNK), CHUNK)
        ]
        wsum[...] = mine.astype(f32) + jnp.sum(wbuf[...].astype(f32), axis=0)
        for d in range(1, n_blk):
            fin_copy(d).start()
        fin[me_b] = wsum[...]

    if owners == n_blk:
        own_chunk()
    else:
        pl.when(me_b < owners)(own_chunk)
    for o in range(owners):
        @pl.when(me_b != o)
        def _():
            remote(wsum, fin.at[o], fin_send.at[0], fin_recv.at[o], me_b, me_r).wait_recv()

        at = o // halves * CHUNK
        gw_ref[at:at + CHUNK, columns(o % halves)] = fin[o]
    results[2].start()

    for c in range(halves):
        swaps[c].wait_send()
        overs[c].wait_send()
        for h in range(2):
            for r in range(n_rep):
                unless(r, lambda: hw_copy(c, h, r).wait_send())
                unless(r, lambda: bw_copy(c, h, r).wait_send())
        for j in range(n_rep):
            pl.when(me_r != j)(lambda: rs_copy(c, j).wait_send())
        for d in range(1, n_rep):
            ag_copy(c, d).wait_send()
    remote(bias_buf, bias_buf, bias_send, bias_recv, me_b, me_r).wait_send()
    if owners == n_blk:
        remote(wbuf, wbuf, w_send, w_recv, me_b, me_r).wait_send()
    else:
        for c in range(halves):
            for g in range(groups):
                for r in range(n_rep):
                    pl.when(me != (g * halves + c) * n_rep + r)(lambda: w_copy(c, g, r).wait_send())

    def fin_left():
        for d in range(1, n_blk):
            fin_copy(d).wait_send()

    if owners == n_blk:
        fin_left()
    else:
        pl.when(me_b < owners)(fin_left)
    for result in results:
        result.wait()


def deliver_kernel(*refs):
    count = len(refs) // 2
    sems = refs[-1]
    copies = [pltpu.make_async_copy(refs[i], refs[count + i], sems.at[i]) for i in range(count)]
    for copy in copies:
        copy.start()
    for copy in copies:
        copy.wait()


def body(feats, weight, bias, grad_out, tile_values, tile_rows, tile_cols, tile_count):
    n_blk = lax.axis_size("blk")
    n_rep = lax.axis_size("rep")
    n_slot, cells, tile = tile_values.shape[2:5]
    rows, width = feats.shape
    n_dev = n_blk * n_rep
    part_rows = rows * n_rep
    side = part_rows // tile
    w_rows = width // n_rep
    owners = (w_rows // CHUNK) * (width // HALF)

    named = tile_rows[0, 0] * side + tile_cols[0, 0]
    live = jnp.arange(cells, dtype=jnp.int32)[None] < tile_count[0, 0][:, None]
    entry = jnp.arange(n_slot * cells, dtype=jnp.int32).reshape(n_slot, cells)
    hit = (named[:, None, :] == jnp.arange(side * side, dtype=jnp.int32)[None, :, None]) & live[:, None, :]
    inv = jnp.min(jnp.where(hit, entry[:, None, :], n_slot * cells), axis=2).reshape(-1)

    assert n_slot == 2 and n_blk == 2 * n_rep
    bf16, f32 = jnp.bfloat16, jnp.float32
    halves = width // HALF
    anywhere = pl.BlockSpec(memory_space=pl.ANY)
    dma = pltpu.SemaphoreType.DMA
    shapes = (
        jax.ShapeDtypeStruct((rows, width), bf16),
        jax.ShapeDtypeStruct((rows, width), bf16),
        jax.ShapeDtypeStruct((w_rows, width), f32),
        jax.ShapeDtypeStruct((1, width), f32),
    )
    results = pl.pallas_call(
        functools.partial(layer_kernel, n_blk, n_rep, n_slot, tile, cells, side),
        out_shape=shapes,
        in_specs=[pl.BlockSpec(memory_space=pltpu.SMEM)] + [anywhere] * 5,
        out_specs=(anywhere,) * 4,
        scratch_shapes=[
            pltpu.VMEM((rows, width), bf16),
            pltpu.VMEM((width, width), bf16),
            pltpu.VMEM((1, width), f32),
            pltpu.VMEM((rows, width), bf16),
            pltpu.VMEM((rows, width), bf16),
            pltpu.VMEM((rows, width), bf16),
            pltpu.VMEM((w_rows, width), f32),
            pltpu.VMEM((1, width), f32),
            pltpu.VMEM((n_slot * cells + 1, tile, tile), bf16),
            pltpu.VMEM((n_slot, part_rows, part_rows), bf16),
            pltpu.VMEM((n_slot, part_rows, part_rows), bf16),
            pltpu.VMEM((halves, rows, HALF), bf16),
            pltpu.VMEM((halves, rows, HALF), bf16),
            pltpu.VMEM((halves, n_slot, n_rep, rows, HALF), bf16),
            pltpu.VMEM((halves, part_rows, HALF), f32),
            pltpu.VMEM((halves, n_rep, rows, HALF), bf16),
            pltpu.VMEM((halves, n_rep, rows, HALF), bf16),
            pltpu.VMEM((halves, n_rep, rows, HALF), bf16),
            pltpu.VMEM((halves, n_slot, n_rep, rows, HALF), bf16),
            pltpu.VMEM((halves, n_slot * n_rep + 1, rows, HALF), bf16),
            pltpu.VMEM((width, rows), bf16),
            pltpu.VMEM((halves, rows, HALF), bf16),
            pltpu.VMEM((8, width), f32),
            pltpu.VMEM((n_blk - 1, 8, width), f32),
            pltpu.VMEM((halves, width, HALF), bf16),
            pltpu.VMEM((n_dev - 1, CHUNK, HALF), bf16),
            pltpu.VMEM((CHUNK, HALF), f32),
            pltpu.VMEM((owners, CHUNK, HALF), f32),
            dma((4,)),
            dma((4,)),
            dma((n_slot,)),
            dma((halves,)),
            dma((halves,)),
            dma((halves,)),
            dma((halves,)),
            dma((halves, n_slot, n_rep)),
            dma((halves, n_slot, n_rep)),
            dma((halves, n_rep)),
            dma((halves, n_rep)),
            dma((halves, n_rep)),
            dma((halves, n_rep)),
            dma((halves, n_slot, n_rep)),
            dma((halves, n_slot * n_rep)),
            dma,
            dma,
            dma,
            dma,
            dma((n_blk,)),
            dma((owners,)),
        ],
        compiler_params=pltpu.CompilerParams(
            collective_id=0, has_side_effects=True, vmem_limit_bytes=56 * 2 ** 20
        ),
        name="graph_layer",
    )(inv, feats, weight, bias.reshape(1, width), grad_out, tile_values.reshape(n_slot * cells, tile, tile))
    out, gf, gw, gb = pl.pallas_call(
        deliver_kernel,
        out_shape=shapes,
        in_specs=[anywhere] * 4,
        out_specs=(anywhere,) * 4,
        scratch_shapes=[dma((4,))],
        name="deliver",
    )(*results)
    return (out, gf, gw, gb.reshape(width))


def solution(mesh):
    in_specs = (
        P(("blk", "rep"), None),
        P(),
        P(),
        P(("blk", "rep"), None),
        P("blk", "rep", None, None, None, None),
        P("blk", "rep", None, None),
        P("blk", "rep", None, None),
        P("blk", "rep", None),
    )
    out_specs = (P(("blk", "rep"), None), P(("blk", "rep"), None), P("rep", None), P())
    return jax.shard_map(body, mesh=mesh, in_specs=in_specs, out_specs=out_specs, check_vma=False)
```

time: 86 us -> 83.4 us (0.970)
  local copies, waits for them, and re-layouts: 6.44 us -> 0.6 us
  Pallas kernels: 77.2 us -> 80.4 us
    pallas_call x0 -> x1, Pallas kernels: none -> 11.1 us  [body(): pl.pallas_call(deliver_kernel, out_shape=shapes, in_specs=[anywhere] * 4,...]
    pallas_call x1, Pallas kernels: 77.2 us -> 69.3 us  [body(): pl.pallas_call(functools.partial(layer_kernel, n_blk, n_rep, n_slot, tile...]
    unnamed x4 -> x0, local copies, waits for them, and re-layouts: 5.84 us -> none
where the time goes in v3:
time: 83.4 us; the launch traced here: 83.2 us
  Pallas kernels  80.4 us (96%)
  other arithmetic  1.54 us (2%)
    pallas_call x1, Pallas kernels, body(): pl.pallas_call(functools.partial(layer_kernel, n_blk, n_rep, n_slot, tile...  69.3 us
    pallas_call x1, Pallas kernels, body(): pl.pallas_call(deliver_kernel, out_shape=shapes, in_specs=[anywhere] * 4,...  11.1 us

profile of v3, /device:TPU:0, one launch (start us, length us, event | category | flops | bytes accessed | tf_op | source)
XLA Modules:
  0.0 83.2 jit_solution(10060839216103718109)
XLA Ops:
  0.6 0.7 iota_compare_fusion.1
  1.4 0.7 add_bitcast_fusion
  2.1 0.1 select_reduce_fusion
  2.2 0.6 reshape.66.inv_ref
  2.8 69.3 %graph_layer.1 = (bf16[256,256]{1,0:T(8,128)(2,1)}, bf16[256,256]{1,0:T(8,128)(2,1)}, f32[64,256]{1,0:T(8,128)}, f32[1,256]{1,0:T(1,128)}) custom-call(s32[128]{0:T(128)} %reshape.66.inv_ref, bf16[256,256]{1,0:T(8,128)(2,1)} %feats_hbm.1, bf16[256,256]{1,0:T(8,128)(2,1)} %weight_hbm.1, f32[1,256]{1,0:T(1,128)} %bitcast.7, bf16[256,256]{1,0:T(8,128)(2,1)} %gout_hbm.1, ...), custom_call_target="tpu_custom_call" | custom-call | tf_op jit(solution)/shard_map/graph_layer/pallas_call | solution.py:394
  72.1 11.1 %deliver.1 = (bf16[256,256]{1,0:T(8,128)(2,1)}, bf16[256,256]{1,0:T(8,128)(2,1)}, f32[64,256]{1,0:T(8,128)}, f32[1,256]{1,0:T(1,128)}) custom-call(bf16[256,256]{1,0:T(8,128)(2,1)} %get-tuple-element.12.refs_0_, bf16[256,256]{1,0:T(8,128)(2,1)} %get-tuple-element.13.refs_1_, f32[64,256]{1,0:T(8,128)} %get-tuple-element.14.refs_2_, ...), custom_call_target="tpu_custom_call" | custom-call | tf_op jit(solution)/shard_map/deliver/pallas_call | solution.py:455
  (1 shorter events, 0.0 us)

commit v4 on v3

--- a/solution.py
+++ b/solution.py
@@ -155,21 +155,20 @@
 
     def forward(c):
         for h in range(2):
-            for u in range(units):
-                for src in range(u * per, (u + 1) * per):
-                    unless(src, lambda: hw_wait(c, h, src))
-                rhs = hwbuf[c, h, u * per:(u + 1) * per].reshape(UNIT, HALF)
-                last = h == 1 and u == units - 1
-                for j in range(units):
-                    at = slice(j * UNIT, (j + 1) * UNIT)
-                    got = jnp.dot(dense[h, at, u * UNIT:(u + 1) * UNIT], rhs, preferred_element_type=f32)
-                    if h + u > 0:
-                        got = got + acc[c, at]
+            for src in range(n_rep):
+                unless(src, lambda: hw_wait(c, h, src))
+            source = hwbuf[c, h].reshape(rows * n_rep, HALF)
+            for j in range(units):
+                at = slice(j * UNIT, (j + 1) * UNIT)
+                got = jnp.dot(dense[h, at], source, preferred_element_type=f32)
+                if h == 0:
                     acc[c, at] = got
-                    if last:
-                        part[c, j * per:(j + 1) * per] = got.astype(bf16).reshape(per, rows, HALF)
-                        for i in range(j * per, (j + 1) * per):
-                            pl.when(me_r != i)(lambda: rs_copy(c, i).start())
+                else:
+                    got = got + acc[c, at]
+                    acc[c, at] = got
+                    part[c, j * per:(j + 1) * per] = got.astype(bf16).reshape(per, rows, HALF)
+                    for i in range(j * per, (j + 1) * per):
+                        pl.when(me_r != i)(lambda: rs_copy(c, i).start())
 
     def ag_copy(c, d):
         to = lax.rem(me_r + d, n_rep)
@@ -355,12 +354,8 @@
 
 def deliver_kernel(*refs):
     count = len(refs) // 2
-    sems = refs[-1]
-    copies = [pltpu.make_async_copy(refs[i], refs[count + i], sems.at[i]) for i in range(count)]
-    for copy in copies:
-        copy.start()
-    for copy in copies:
-        copy.wait()
+    for src, dst in zip(refs[:count], refs[count:]):
+        dst[...] = src[...]
 
 
 def body(feats, weight, bias, grad_out, tile_values, tile_rows, tile_cols, tile_count):
@@ -383,6 +378,7 @@
     assert n_slot == 2 and n_blk == 2 * n_rep
     bf16, f32 = jnp.bfloat16, jnp.float32
     halves = width // HALF
+    vmem = pl.BlockSpec(memory_space=pltpu.VMEM)
     anywhere = pl.BlockSpec(memory_space=pl.ANY)
     dma = pltpu.SemaphoreType.DMA
     shapes = (
@@ -455,9 +451,8 @@
     out, gf, gw, gb = pl.pallas_call(
         deliver_kernel,
         out_shape=shapes,
-        in_specs=[anywhere] * 4,
-        out_specs=(anywhere,) * 4,
-        scratch_shapes=[dma((4,))],
+        in_specs=[vmem] * 4,
+        out_specs=(vmem,) * 4,
         name="deliver",
     )(*results)
     return (out, gf, gw, gb.reshape(width))

time: 83.4 us -> 73.6 us (0.88)
  Pallas kernels: 80.4 us -> 70.6 us
    pallas_call x1, Pallas kernels: 11.1 us -> 1.7 us  [body(): pl.pallas_call(deliver_kernel, out_shape=shapes, in_specs=[vmem] * 4, out...]
where the time goes in v4:
time: 73.6 us; the launch traced here: 73.4 us
  Pallas kernels  70.6 us (96%)
  other arithmetic  1.54 us (2%)
    pallas_call x1, Pallas kernels, body(): pl.pallas_call(functools.partial(layer_kernel, n_blk, n_rep, n_slot, tile...  68.9 us
    pallas_call x1, Pallas kernels, body(): pl.pallas_call(deliver_kernel, out_shape=shapes, in_specs=[vmem] * 4, out...  1.7 us

profile of v4, /device:TPU:0, one launch (start us, length us, event | category | flops | bytes accessed | tf_op | source)
XLA Modules:
  0.0 73.4 jit_solution(13100218108212492000)
XLA Ops:
  0.6 0.7 iota_compare_fusion.1
  1.4 0.7 add_bitcast_fusion
  2.1 0.1 select_reduce_fusion
  2.2 0.6 reshape.66.inv_ref
  2.8 68.9 %graph_layer.1 = (bf16[256,256]{1,0:T(8,128)(2,1)}, bf16[256,256]{1,0:T(8,128)(2,1)}, f32[64,256]{1,0:T(8,128)}, f32[1,256]{1,0:T(1,128)}) custom-call(s32[128]{0:T(128)} %reshape.66.inv_ref, bf16[256,256]{1,0:T(8,128)(2,1)} %feats_hbm.1, bf16[256,256]{1,0:T(8,128)(2,1)} %weight_hbm.1, f32[1,256]{1,0:T(1,128)} %bitcast.7, bf16[256,256]{1,0:T(8,128)(2,1)} %gout_hbm.1, ...), custom_call_target="tpu_custom_call" | custom-call | tf_op jit(solution)/shard_map/graph_layer/pallas_call | solution.py:390
  71.7 1.7 %deliver.1 = (bf16[256,256]{1,0:T(8,128)(2,1)}, bf16[256,256]{1,0:T(8,128)(2,1)}, f32[64,256]{1,0:T(8,128)}, f32[1,256]{1,0:T(1,128)}) custom-call(bf16[256,256]{1,0:T(8,128)(2,1)} %get-tuple-element.12.refs_0_, bf16[256,256]{1,0:T(8,128)(2,1)} %get-tuple-element.13.refs_1_, f32[64,256]{1,0:T(8,128)} %get-tuple-element.14.refs_2_, ...), custom_call_target="tpu_custom_call" | custom-call | tf_op jit(solution)/shard_map/deliver/pallas_call | solution.py:451
  (1 shorter events, 0.0 us)

commit v5 on v4

--- a/solution.py
+++ b/solution.py
@@ -21,12 +21,12 @@
 
 def layer_kernel(
     n_blk, n_rep, n_slot, tile, cells, tiles_side,
-    inv_ref, feats_hbm, weight_hbm, bias_hbm, gout_hbm, tiles_hbm,
+    count_ref, rows_hbm, cols_hbm, feats_hbm, weight_hbm, bias_hbm, gout_hbm, tiles_hbm,
     out_hbm, gf_hbm, gw_hbm, gb_hbm,
-    feats_ref, weight_ref, bias_ref, gout_ref, out_ref, gf_ref, gw_ref, gb_ref,
+    rows_ref, cols_ref, inv_vec, inv_ref, feats_ref, weight_ref, bias_ref, gout_ref, out_ref, gf_ref, gw_ref, gb_ref,
     tiles, dense, dense_t, hw, hw_other, hwbuf, acc, part, aggbuf, gbuf, pbuf, ghbuf, feats_t,
     cross, bias_mine, bias_buf, terms, wbuf, wsum, fin,
-    in_sem, out_sem, tile_sem, swap_send, swap_recv, cross_send, cross_recv, hw_send, hw_recv,
+    in_sem, index_sem, out_sem, tile_sem, swap_send, swap_recv, cross_send, cross_recv, hw_send, hw_recv,
     rs_send, rs_recv, ag_send, ag_recv, bw_send, bw_recv,
     bias_send, bias_recv, w_send, w_recv, fin_send, fin_recv,
 ):
@@ -56,6 +56,12 @@
         else:
             task()
 
+    index_in = [
+        pltpu.make_async_copy(rows_hbm, rows_ref, index_sem.at[0]),
+        pltpu.make_async_copy(cols_hbm, cols_ref, index_sem.at[1]),
+    ]
+    for copy in index_in:
+        copy.start()
     small = []
     for i, (src, dst) in enumerate(
         ((feats_hbm, feats_ref), (weight_hbm, weight_ref), (bias_hbm, bias_ref), (gout_hbm, gout_ref))
@@ -84,6 +90,21 @@
     first = jnp.dot(feats_ref[...], weight_ref[...], preferred_element_type=f32).astype(bf16)
     for c in range(halves):
         hw[c] = first[:, columns(c)]
+
+    for copy in index_in:
+        copy.wait()
+    for k in range(n_slot):
+        named = rows_ref[k:k + 1] * tiles_side + cols_ref[k:k + 1]
+        position = lax.broadcasted_iota(jnp.int32, (1, cells), 1)
+        named = jnp.where(position < count_ref[k], named, -1)
+        named = jnp.concatenate([named] * (HALF // cells), axis=1)
+        by_entry = jnp.broadcast_to(named, (HALF, HALF)).T
+        entry = lax.broadcasted_iota(jnp.int32, (HALF, HALF), 0)
+        cell = lax.broadcasted_iota(jnp.int32, (HALF, HALF), 1)
+        found = jnp.where(by_entry == cell, lax.rem(entry, cells) + k * cells, n_slot * cells)
+        inv_vec[k:k + 1] = jnp.min(found, axis=0, keepdims=True)
+    to_scalars = pltpu.make_async_copy(inv_vec, inv_ref, index_sem.at[2])
+    to_scalars.start()
     pl.semaphore_wait(barrier, n_dev - 1)
 
     swaps = [
@@ -104,23 +125,23 @@
             hwbuf[c, h, 0] = hw[c] if h == 0 else hw_other[c]
 
     def fill(h):
-        base = jnp.where(near_slot == 1, 1 - h, h) * tiles_side * tiles_side
+        slot = jnp.where(near_slot == 1, 1 - h, h)
 
         def fill_rows(r, carry):
             at = pl.ds(pl.multiple_of(r * tile, tile), tile)
             for c in range(tiles_side):
-                dense[h, at, c * tile:(c + 1) * tile] = tiles[inv_ref[base + r * tiles_side + c]]
+                dense[h, at, c * tile:(c + 1) * tile] = tiles[inv_ref[slot, r * tiles_side + c]]
             return carry
 
         lax.fori_loop(0, tiles_side, fill_rows, 0)
 
     def fill_transposed(h):
-        base = jnp.where(near_slot == 1, 1 - h, h) * tiles_side * tiles_side
+        slot = jnp.where(near_slot == 1, 1 - h, h)
 
         def fill_rows(c, carry):
             at = pl.ds(pl.multiple_of(c * tile, tile), tile)
             for r in range(tiles_side):
-                dense_t[h, at, r * tile:(r + 1) * tile] = tiles[inv_ref[base + r * tiles_side + c]].T
+                dense_t[h, at, r * tile:(r + 1) * tile] = tiles[inv_ref[slot, r * tiles_side + c]].T
             return carry
 
         lax.fori_loop(0, tiles_side, fill_rows, 0)
@@ -132,6 +153,7 @@
     tiles[n_slot * cells] = jnp.zeros((tile, tile), bf16)
     for load in loads:
         load.wait()
+    to_scalars.wait()
     fill(0)
     swaps[0].wait_recv()
     hw_share(0, 1)
@@ -142,8 +164,6 @@
         swaps[c].wait_recv()
         hw_share(c, 1)
     fill_transposed(1)
-    fill_transposed(0)
-    feats_t[...] = feats_ref[...].T
 
     def hw_wait(c, h, src):
         remote(
@@ -261,6 +281,9 @@
 
     for c in range(halves):
         forward(c)
+        if c == 0:
+            fill_transposed(0)
+            feats_t[...] = feats_ref[...].T
     small[2].wait()
     small[3].wait()
     for c in range(halves):
@@ -369,13 +392,7 @@
     w_rows = width // n_rep
     owners = (w_rows // CHUNK) * (width // HALF)
 
-    named = tile_rows[0, 0] * side + tile_cols[0, 0]
-    live = jnp.arange(cells, dtype=jnp.int32)[None] < tile_count[0, 0][:, None]
-    entry = jnp.arange(n_slot * cells, dtype=jnp.int32).reshape(n_slot, cells)
-    hit = (named[:, None, :] == jnp.arange(side * side, dtype=jnp.int32)[None, :, None]) & live[:, None, :]
-    inv = jnp.min(jnp.where(hit, entry[:, None, :], n_slot * cells), axis=2).reshape(-1)
-
-    assert n_slot == 2 and n_blk == 2 * n_rep
+    assert n_slot == 2 and n_blk == 2 * n_rep and HALF % cells == 0 and side * side <= HALF
     bf16, f32 = jnp.bfloat16, jnp.float32
     halves = width // HALF
     vmem = pl.BlockSpec(memory_space=pltpu.VMEM)
@@ -390,9 +407,13 @@
     results = pl.pallas_call(
         functools.partial(layer_kernel, n_blk, n_rep, n_slot, tile, cells, side),
         out_shape=shapes,
-        in_specs=[pl.BlockSpec(memory_space=pltpu.SMEM)] + [anywhere] * 5,
+        in_specs=[pl.BlockSpec(memory_space=pltpu.SMEM)] + [anywhere] * 7,
         out_specs=(anywhere,) * 4,
         scratch_shapes=[
+            pltpu.VMEM((n_slot, cells), jnp.int32),
+            pltpu.VMEM((n_slot, cells), jnp.int32),
+            pltpu.VMEM((n_slot, HALF), jnp.int32),
+            pltpu.SMEM((n_slot, HALF), jnp.int32),
             pltpu.VMEM((rows, width), bf16),
             pltpu.VMEM((width, width), bf16),
             pltpu.VMEM((1, width), f32),
@@ -422,6 +443,7 @@
             pltpu.VMEM((CHUNK, HALF), f32),
             pltpu.VMEM((owners, CHUNK, HALF), f32),
             dma((4,)),
+            dma((3,)),
             dma((4,)),
             dma((n_slot,)),
             dma((halves,)),
@@ -447,7 +469,10 @@
             collective_id=0, has_side_effects=True, vmem_limit_bytes=56 * 2 ** 20
         ),
         name="graph_layer",
-    )(inv, feats, weight, bias.reshape(1, width), grad_out, tile_values.reshape(n_slot * cells, tile, tile))
+    )(
+        tile_count[0, 0], tile_rows[0, 0], tile_cols[0, 0], feats, weight, bias.reshape(1, width), grad_out,
+        tile_values.reshape(n_slot * cells, tile, tile),
+    )
     out, gf, gw, gb = pl.pallas_call(
         deliver_kernel,
         out_shape=shapes,

time: 73.6 us -> 71.8 us (0.976)
  other arithmetic: 1.54 us -> 0 us
where the time goes in v5:
time: 71.8 us; the launch traced here: 71.6 us
  Pallas kernels  71 us (99%)
    pallas_call x1, Pallas kernels, body(): pl.pallas_call(functools.partial(layer_kernel, n_blk, n_rep, n_slot, tile...  69.3 us
    pallas_call x1, Pallas kernels, body(): pl.pallas_call(deliver_kernel, out_shape=shapes, in_specs=[vmem] * 4, out...  1.7 us

profile of v5, /device:TPU:0, one launch (start us, length us, event | category | flops | bytes accessed | tf_op | source)
XLA Modules:
  0.0 71.6 jit_solution(8207431646449030944)
XLA Ops:
  0.6 69.3 %graph_layer.1 = (bf16[256,256]{1,0:T(8,128)(2,1)}, bf16[256,256]{1,0:T(8,128)(2,1)}, f32[64,256]{1,0:T(8,128)}, f32[1,256]{1,0:T(1,128)}) custom-call(s32[2]{0:T(128)} %bitcast.10, s32[2,64]{1,0:T(2,128)} %bitcast.7, s32[2,64]{1,0:T(2,128)} %bitcast.8, bf16[256,256]{1,0:T(8,128)(2,1)} %feats_hbm.1, bf16[256,256]{1,0:T(8,128)(2,1)} %weight_hbm.1, ...), custom_call_target="tpu_custom_call" | custom-call | tf_op jit(solution)/shard_map/graph_layer/pallas_call | solution.py:407
  69.9 1.7 %deliver.1 = (bf16[256,256]{1,0:T(8,128)(2,1)}, bf16[256,256]{1,0:T(8,128)(2,1)}, f32[64,256]{1,0:T(8,128)}, f32[1,256]{1,0:T(1,128)}) custom-call(bf16[256,256]{1,0:T(8,128)(2,1)} %get-tuple-element.12.refs_0_, bf16[256,256]{1,0:T(8,128)(2,1)} %get-tuple-element.13.refs_1_, f32[64,256]{1,0:T(8,128)} %get-tuple-element.14.refs_2_, ...), custom_call_target="tpu_custom_call" | custom-call | tf_op jit(solution)/shard_map/deliver/pallas_call | solution.py:476
